TPU v7x, 128 devices: a whole 4x4x4 slice. The times are simulated.
128 devices in a mesh: expert: 16 (over x, z), dp: 8 (over y, core).
Axes of the slice: x: 4, y: 4, z: 4, core: 2. Of those that a mesh axis runs over, the one named last changes fastest.
Arguments:
- tokens: bfloat16 [20480, 2048], P(('expert', 'dp')), may hold values from -6 to 6
- expert_ids: int32 [20480, 2], P(('expert', 'dp')), may hold values from 0 to 63, as said below
- gate_weights: float32 [20480, 2], P(('expert', 'dp')), may hold values from 0.1 to 1
- grad_output: bfloat16 [20480, 2048], P(('expert', 'dp')), may hold values from -6 to 6
- gate_weight: bfloat16 [128, 768, 2048], P(('expert', 'dp')), may hold values from -0.125 to 0.125
- up_weight: bfloat16 [128, 768, 2048], P(('expert', 'dp')), may hold values from -0.125 to 0.125
- down_weight: bfloat16 [128, 768, 2048], P(('expert', 'dp')), may hold values from -0.15625 to 0.15625
- swap_slot: int32 [8], replicated, may hold values from 0 to 3
- slot_cap: int32 [16, 4], replicated, may hold values from 2 to 5
Outputs:
- layer_out: bfloat16 [20480, 2048], P(('expert', 'dp'))
- grad_tokens: bfloat16 [20480, 2048], P(('expert', 'dp'))
- grad_routing: float32 [20480, 2], P(('expert', 'dp'))
- gate_grad: bfloat16 [128, 768, 2048], P(('expert', 'dp'))
- up_grad: bfloat16 [128, 768, 2048], P(('expert', 'dp'))
- down_grad: bfloat16 [128, 768, 2048], P(('expert', 'dp'))
Inputs may be any that keep to these rules, and one draw needn't show every extreme that they name: `expert_ids`: in the rows of one device (aligned blocks of 160 rows) each expert is named by exactly 5 rows, and each row names 2 different experts.
All inputs are finite; a program needn't handle non-finite values.
Results may differ from a plain program's by a relative error of at most 0.0071.
Values may be sent and summed in bfloat16 or wider, within the bound.
A program may use at most 128 MiB of HBM per device.

v0:
```python
import functools

import jax
import jax.numpy as jnp
from jax import lax
from jax.experimental import pallas as pl
from jax.experimental.pallas import tpu as pltpu
from jax.sharding import PartitionSpec as P

BF = jnp.bfloat16
F32 = jnp.float32
MESH = pl.DeviceIdType.MESH
SIDE = 4
CHIPS = SIDE**3
LANES = 128
NT = (((1,), (1,)), ((), ()))
NN = (((1,), (0,)), ((), ()))


def dot(a, b, dims):
    return lax.dot_general(a, b, dims, preferred_element_type=F32)


def offset_of(n):
    n2, n1, n0 = n // 16, (n // 4) % 4, n % 4
    return n1, n0, (n2 + n1 + n0) % 4


def kernel(groups, cap, idx, gate_q, row_of, gate_a, tok, grad, wg_hbm, wu_hbm, wd_hbm,
           lo, gt, gr, gg_hbm, ug_hbm, dg_hbm,
           send, recv, xs, ds, act, dgate, dup, scr_a, scr_b, own, other, part, ret,
           wg, wu, wd, act_t, dgate_t, dup_t, stage,
           send_sem, recv_sem, fwd_ssem, fwd_rsem, part_ssem, part_rsem, ret_ssem, ret_rsem, w_sem, out_sem):
    width = wg.shape[1]
    units = wg.shape[0]
    cols = width // LANES
    tokens = tok.shape[0]
    slots = CHIPS // groups
    half = slots * cap
    rows = 2 * half

    h = lax.axis_index("expert")
    d = lax.axis_index("dp")
    x, z, y, c = h // SIDE, h % SIDE, d // 2, d % 2
    sibling = {"expert": h, "dp": y * 2 + (1 - c)}

    def chip(n, sign):
        kx, kz, ky = offset_of(n)
        if sign < 0:
            kx, kz, ky = SIDE - kx, SIDE - kz, SIDE - ky
        return {"expert": ((x + kx) % SIDE) * SIDE + (z + kz) % SIDE, "dp": ((y + ky) % SIDE) * 2 + c}

    barrier = pltpu.get_barrier_semaphore()
    pl.semaphore_signal(barrier, inc=1, device_id=sibling, device_id_type=MESH)

    def greet(n, _):
        pl.semaphore_signal(barrier, inc=1, device_id=chip(n, 1), device_id_type=MESH)
        return 0

    lax.fori_loop(1, CHIPS, greet, 0)

    def weight_copy(i):
        return pltpu.make_async_copy((wg_hbm, wu_hbm, wd_hbm)[i].at[0], (wg, wu, wd)[i], w_sem.at[i])

    for i in range(3):
        weight_copy(i).start()

    def dispatch(n):
        return pltpu.make_async_remote_copy(
            src_ref=send.at[n], dst_ref=recv.at[0, n], send_sem=send_sem.at[n], recv_sem=recv_sem.at[n],
            device_id=chip(n, 1), device_id_type=MESH)

    def gather(n, put):
        for r in range(cap):
            q = n * cap + r
            t = idx[q]
            put(r, tok[t])
            put(cap + r, (gate_q[q] * grad[t].astype(F32)).astype(BF))

    def put_own(r, value):
        recv[0, 0, r] = value

    gather(0, put_own)

    pl.semaphore_wait(barrier, CHIPS)

    def send_rows(n, _):
        def put(r, value):
            send[n, r] = value
        gather(n, put)
        dispatch(n).start()
        return 0

    lax.fori_loop(1, CHIPS, send_rows, 0)

    def forward(g):
        at = pl.ds(g * slots, slots)
        return pltpu.make_async_remote_copy(
            src_ref=recv.at[0, at], dst_ref=recv.at[1, at], send_sem=fwd_ssem.at[g], recv_sem=fwd_rsem.at[g],
            device_id=sibling, device_id_type=MESH)

    def trade(g):
        at = pl.ds(g * slots, slots)
        return pltpu.make_async_remote_copy(
            src_ref=other.at[at], dst_ref=part.at[at], send_sem=part_ssem.at[g], recv_sem=part_rsem.at[g],
            device_id=sibling, device_id_type=MESH)

    def give_back(n):
        return pltpu.make_async_remote_copy(
            src_ref=own.at[n], dst_ref=ret.at[n], send_sem=ret_ssem.at[n], recv_sem=ret_rsem.at[n],
            device_id=chip(n, -1), device_id_type=MESH)

    def arrive(g):
        def one(n, _):
            dispatch(n).wait_recv()
            return 0
        lax.fori_loop(max(g * slots, 1), (g + 1) * slots, one, 0)
        forward(g).start()

    def compute(g):
        base = g * rows
        first = g * slots
        forward(g).wait_recv()
        if g == 0:
            for i in range(3):
                weight_copy(i).wait()
        for p in range(2):
            def spread(i, _):
                n0 = first + i * 16
                r0 = pl.multiple_of(base + p * half + i * 16 * cap, 16)
                for lo_row, scr, dst in ((0, scr_a, xs), (cap, scr_b, ds)):
                    value = recv[p, pl.ds(n0, 16), lo_row:lo_row + cap].astype(F32)
                    scr[pl.ds(0, 16 * cap * cols), :] = value.reshape(16 * cap * cols, LANES)
                    for j in range(cols):
                        dst[pl.ds(r0, 16 * cap), j * LANES:(j + 1) * LANES] = scr[
                            pl.ds(j, 16 * cap, stride=cols), :].astype(BF)
                return 0
            lax.fori_loop(0, slots // 16, spread, 0)
        here = pl.ds(base, rows)

        def hidden(n, _):
            f = pl.ds(pl.multiple_of(n * 256, 256), 256)
            gate_pre = dot(xs[here, :], wg[f, :], NT)
            up_pre = dot(xs[here, :], wu[f, :], NT)
            grad_act = dot(ds[here, :], wd[f, :], NT)
            sig = jax.nn.sigmoid(gate_pre)
            silu = gate_pre * sig
            act[here, f] = (silu * up_pre).astype(BF)
            dup[here, f] = (grad_act * silu).astype(BF)
            dgate[here, f] = (grad_act * up_pre * sig * (1.0 + gate_pre * (1.0 - sig))).astype(BF)
            return 0

        lax.fori_loop(0, units // 256, hidden, 0)

        def model(n, _):
            f = pl.ds(pl.multiple_of(n * 256, 256), 256)
            out = dot(act[here, :], wd[:, f], NN)
            back = dot(dgate[here, :], wg[:, f], NN) + dot(dup[here, :], wu[:, f], NN)
            for k in range(2):
                lanes = slice(k * LANES, (k + 1) * LANES)
                scr_a[pl.ds(n * 2 + k, rows, stride=cols), :] = out[:, lanes]
                scr_b[pl.ds(n * 2 + k, rows, stride=cols), :] = back[:, lanes]
            return 0

        lax.fori_loop(0, width // 256, model, 0)
        for p, dst in ((0, own), (1, other)):
            def pack(i, _):
                n0 = first + i * 16
                at = pl.ds(pl.multiple_of((p * half + i * 16 * cap) * cols, 16), 16 * cap * cols)
                for lo_row, scr in ((0, scr_a), (cap, scr_b)):
                    dst[pl.ds(n0, 16), lo_row:lo_row + cap] = scr[at, :].astype(BF).reshape(16, cap, cols, LANES)
                return 0
            lax.fori_loop(0, slots // 16, pack, 0)
        trade(g).start()

    def finish(g):
        trade(g).wait_recv()

        def one(n, _):
            total = (own[n].astype(F32) + part[n].astype(F32)).astype(BF)
            own[n] = total
            give_back(n).start()
            return 0

        if g == 0:
            ret[0] = (own[0].astype(F32) + part[0].astype(F32)).astype(BF)
        lax.fori_loop(max(g * slots, 1), (g + 1) * slots, one, 0)

    for step in range(groups + 2):
        if step < groups:
            arrive(step)
        if 1 <= step <= groups:
            compute(step - 1)
        if step >= 2:
            finish(step - 2)

    act_t[...] = act[...].T
    dgate_t[...] = dgate[...].T
    dup_t[...] = dup[...].T
    tile = stage.shape[3]

    def out_copy(i, k, n):
        return pltpu.make_async_copy(
            stage.at[k, i],
            (gg_hbm, ug_hbm, dg_hbm)[i].at[0, :, pl.ds(pl.multiple_of(n * tile, tile), tile)],
            out_sem.at[k, i])

    steps = width // tile
    for n in range(steps):
        k = n % 2
        f = slice(n * tile, (n + 1) * tile)
        for i, (left, right) in enumerate(((dgate_t, xs), (dup_t, xs), (act_t, ds))):
            if n >= 2:
                out_copy(i, k, n - 2).wait()
            stage[k, i] = dot(left[...], right[:, f], NN).astype(BF)
            out_copy(i, k, n).start()

    def drain(n, _):
        give_back(n).wait_recv()
        return 0

    lax.fori_loop(1, CHIPS, drain, 0)

    def combine(t, _):
        cot = grad[t].astype(F32)
        total = jnp.zeros((cols, LANES), F32)
        back = jnp.zeros((cols, LANES), F32)
        for k in range(2):
            a = 2 * t + k
            q = row_of[a]
            n = q // (2 * cap)
            r = q % (2 * cap)
            out_row = ret[n, r].astype(F32)
            total = total + gate_a[a] * out_row
            back = back + ret[n, r + cap].astype(F32)
            gr[pl.ds(a, 1), :] = jnp.sum(cot * out_row, axis=0, keepdims=True)
        lo[t] = total.astype(BF)
        gt[t] = back.astype(BF)
        return 0

    lax.fori_loop(0, tokens, combine, 0)

    def settle(n, _):
        dispatch(n).wait_send()
        give_back(n).wait_send()
        return 0

    lax.fori_loop(1, CHIPS, settle, 0)
    for g in range(groups):
        forward(g).wait_send()
        trade(g).wait_send()
    for n in range(max(steps - 2, 0), steps):
        for i in range(3):
            out_copy(i, n % 2, n).wait()


def body(tokens, expert_ids, gate_weights, grad_output, gate_weight, up_weight, down_weight, swap_slot, slot_cap):
    count, top = expert_ids.shape
    width = tokens.shape[1]
    units = gate_weight.shape[1]
    holders, per = slot_cap.shape
    experts = holders * per
    cap = count * top // experts
    assigns = count * top
    cols = width // LANES
    groups = 2
    slots = CHIPS // groups
    rows = 2 * slots * cap

    h = lax.axis_index("expert")
    d = lax.axis_index("dp")
    half = holders // 2
    moved = jnp.concatenate([swap_slot, swap_slot])[:, None] == jnp.arange(per, dtype=jnp.int32)[None, :]
    rolled = jnp.concatenate([slot_cap[half:], slot_cap[:half]], axis=0)
    capacity = jnp.where(moved, rolled, slot_cap).reshape(experts)
    ids = expert_ids.reshape(-1)
    gates = gate_weights.reshape(-1)
    a_range = jnp.arange(assigns, dtype=jnp.int32)
    rank = jnp.sum(((ids[:, None] == ids[None, :]) & (a_range[None, :] < a_range[:, None])).astype(jnp.int32), axis=1)
    my_cap = jnp.sum(
        jnp.where(ids[:, None] == jnp.arange(experts, dtype=jnp.int32)[None, :], capacity[None, :], 0), axis=1)
    kept = rank < my_cap
    kx = (ids // 16 + SIDE - h // SIDE) % SIDE
    kz = ((ids // 4) % 4 + SIDE - h % SIDE) % SIDE
    ky = (ids % 4 + SIDE - d // 2) % SIDE
    slot = ((ky + 2 * SIDE - kx - kz) % SIDE) * 16 + kx * 4 + kz
    position = slot * cap + rank
    row_of = slot * 2 * cap + rank
    gate_a = jnp.where(kept, gates, 0.0)
    match = position[None, :] == a_range[:, None]
    idx = jnp.sum(jnp.where(match, (a_range // top)[None, :], 0), axis=1)
    gate_q = jnp.sum(jnp.where(match, gate_a[None, :], 0.0), axis=1)

    smem = pl.BlockSpec(memory_space=pltpu.SMEM)
    vmem = pl.BlockSpec(memory_space=pltpu.VMEM)
    hbm = pl.BlockSpec(memory_space=pl.ANY)
    rows3 = jax.ShapeDtypeStruct((count, cols, LANES), BF)
    block = (CHIPS, 2 * cap, cols, LANES)
    total = 2 * CHIPS * cap
    weights = jax.ShapeDtypeStruct((1, units, width), BF)
    dma = pltpu.SemaphoreType.DMA
    lo, gt, gr, gg, ug, dg = pl.pallas_call(
        functools.partial(kernel, groups, cap),
        out_shape=(rows3, rows3, jax.ShapeDtypeStruct((assigns, LANES), F32), weights, weights, weights),
        in_specs=[smem] * 4 + [vmem] * 2 + [hbm] * 3,
        out_specs=(vmem, vmem, vmem, hbm, hbm, hbm),
        scratch_shapes=[
            pltpu.VMEM(block, BF),
            pltpu.VMEM((2,) + block, BF),
            pltpu.VMEM((total, width), BF),
            pltpu.VMEM((total, width), BF),
            pltpu.VMEM((total, units), BF),
            pltpu.VMEM((total, units), BF),
            pltpu.VMEM((total, units), BF),
            pltpu.VMEM((rows * cols, LANES), F32),
            pltpu.VMEM((rows * cols, LANES), F32),
            pltpu.VMEM(block, BF),
            pltpu.VMEM(block, BF),
            pltpu.VMEM(block, BF),
            pltpu.VMEM(block, BF),
            pltpu.VMEM((units, width), BF),
            pltpu.VMEM((units, width), BF),
            pltpu.VMEM((units, width), BF),
            pltpu.VMEM((units, total), BF),
            pltpu.VMEM((units, total), BF),
            pltpu.VMEM((units, total), BF),
            pltpu.VMEM((2, 3, units, 256), BF),
            dma((CHIPS,)),
            dma((CHIPS,)),
            dma((groups,)),
            dma((groups,)),
            dma((groups,)),
            dma((groups,)),
            dma((CHIPS,)),
            dma((CHIPS,)),
            dma((3,)),
            dma((2, 3)),
        ],
        compiler_params=pltpu.CompilerParams(
            collective_id=0, has_side_effects=True, vmem_limit_bytes=62 * 1024 * 1024),
        cost_estimate=pl.CostEstimate(
            flops=18 * total * units * width, bytes_accessed=12 * units * width, transcendentals=0),
    )(idx, gate_q, row_of, gate_a, tokens.reshape(count, cols, LANES), grad_output.reshape(count, cols, LANES),
      gate_weight, up_weight, down_weight)
    routing = jnp.where(kept, jnp.sum(gr, axis=1), 0.0).reshape(count, top)
    return lo.reshape(count, width), gt.reshape(count, width), routing, gg, ug, dg


def solution(mesh):
    flat = P(("expert", "dp"), None)
    cube = P(("expert", "dp"), None, None)
    return jax.shard_map(
        body,
        mesh=mesh,
        in_specs=(flat, flat, flat, flat, cube, cube, cube, P(), P()),
        out_specs=(flat, flat, flat, cube, cube, cube),
        check_vma=False,
    )
```

profile of v0, /device:TPU:1, one launch (start us, length us, event | category | flops | bytes accessed | tf_op | source)
XLA Modules:
  0.0 134.9 jit_solution(12686389400168524685)
XLA Ops:
  0.7 0.8 pad_add_fusion
  1.5 0.8 fusion.24
  2.3 0.8 add_select_fusion.9
  3.1 0.1 copy.21
  3.1 0.1 broadcast_in_dim.54
  3.2 0.8 copy.20
  4.0 0.1 reshape.194
  4.2 0.1 select_reduce_fusion.2
  4.3 0.2 convert_reduce_fusion
  4.5 0.6 multiply_add_fusion
  5.1 0.7 select_reduce_fusion.1.idx
  5.8 0.8 copy.22
  6.6 0.1 reshape.195
  6.8 0.0 copy-start.2
  6.8 0.7 select_reduce_fusion.gate_q
  7.5 2.1 %copy.24 = bf16[20,8,16,128]{3,2,1,0:T(8,128)(2,1)} copy(bf16[20,8,16,128]{3,1,2,0:T(8,128)(2,1)} %bitcast.12) | data formatting | bytes 1310720
  9.6 2.1 %copy.25 = bf16[20,8,16,128]{3,2,1,0:T(8,128)(2,1)} copy(bf16[20,8,16,128]{3,1,2,0:T(8,128)(2,1)} %bitcast.13) | data formatting | bytes 1310720
  11.7 0.0 copy-done.2
  11.7 108.4 %shard_map.136 = (bf16[160,16,128]{2,1,0:T(8,128)(2,1)}, bf16[160,16,128]{2,1,0:T(8,128)(2,1)}, f32[320,128]{1,0:T(8,128)}, bf16[1,768,2048]{2,1,0:T(8,128)(2,1)...) custom-call(s32[320]{0:T(512)} %select_reduce_fusion.1.idx, f32[320]{0:T(512)} %select_reduce_fusion.gate_q, ...), custom_call_target="tpu_custom_call" | custom-call | flops 18119393280 | bytes 18874368 | tf_op jit(solution)/shard_map/pallas_call | solution.py:302
  120.1 2.1 %copy.31 = bf16[20,8,16,128]{3,1,2,0:T(8,128)(2,1)} copy(bf16[20,8,16,128]{3,2,1,0:T(8,128)(2,1)} %bitcast.17) | data formatting | bytes 1310720
  122.1 2.1 %copy.30 = bf16[20,8,16,128]{3,1,2,0:T(8,128)(2,1)} copy(bf16[20,8,16,128]{3,2,1,0:T(8,128)(2,1)} %bitcast.16) | data formatting | bytes 1310720
  124.2 1.1 reduce_sum.49
  125.3 0.1 select_n.132
  125.5 0.7 copy.23
  126.1 0.0 copy-start.1
  126.1 4.1 %copy.35 = bf16[1,768,2048]{2,1,0:T(8,128)(2,1)} copy(bf16[1,768,2048]{2,1,0:T(8,128)(2,1)} %get-tuple-element.47) | data formatting | bytes 6291456
  130.2 0.0 copy-done.1
  130.2 0.0 copy-start
  130.2 1.7 %copy.36 = bf16[1,768,2048]{2,1,0:T(8,128)(2,1)} copy(bf16[1,768,2048]{2,1,0:T(8,128)(2,1)S(1)} %copy-done.1) | data formatting | bytes 6291456
  131.9 1.4 %copy-done = bf16[1,768,2048]{2,1,0:T(8,128)(2,1)S(1)} copy-done((bf16[1,768,2048]{2,1,0:T(8,128)(2,1)S(1)}, bf16[1,768,2048]{2,1,0:T(8,128)(2,1)}, u32[]{:S(2)}) %copy-start) | copy-done | bytes 3145752
  133.3 1.7 %copy.37 = bf16[1,768,2048]{2,1,0:T(8,128)(2,1)} copy(bf16[1,768,2048]{2,1,0:T(8,128)(2,1)S(1)} %copy-done) | data formatting | bytes 6291456
  (3 shorter events, 0.0 us)
Async XLA Ops:
  6.8 4.9 %copy-start.2 = (f32[320]{0:T(512)}, f32[320]{0:T(512)S(1)}, u32[]{:S(2)}) copy-start(f32[320]{0:T(512)S(1)} %get-tuple-element.32.gate_a) | copy-start | bytes 3844
  126.1 4.1 %copy-start.1 = (bf16[1,768,2048]{2,1,0:T(8,128)(2,1)S(1)}, bf16[1,768,2048]{2,1,0:T(8,128)(2,1)}, u32[]{:S(2)}) copy-start(bf16[1,768,2048]{2,1,0:T(8,128)(2,1)} %get-tuple-element.48) | copy-start | bytes 9437188
  130.2 3.0 %copy-start = (bf16[1,768,2048]{2,1,0:T(8,128)(2,1)S(1)}, bf16[1,768,2048]{2,1,0:T(8,128)(2,1)}, u32[]{:S(2)}) copy-start(bf16[1,768,2048]{2,1,0:T(8,128)(2,1)} %get-tuple-element.49) | copy-start | bytes 9437188
where the time goes:
time: 135 us
  Pallas kernels  108 us (80%)
  local copies, waits for them, and re-layouts  20.8 us (15%)
  other arithmetic  5.05 us (4%)
    pallas_call x1, Pallas kernels, body(): pl.pallas_call(functools.partial(kernel, groups, cap), out_shape=(rows3,...  108 us
    unnamed x16, local copies, waits for them, and re-layouts  19.4 us

commit v1 on v0

--- a/solution.py
+++ b/solution.py
@@ -26,15 +26,58 @@
     return n1, n0, (n2 + n1 + n0) % 4
 
 
-def kernel(groups, cap, idx, gate_q, row_of, gate_a, tok, grad, wg_hbm, wu_hbm, wd_hbm,
-           lo, gt, gr, gg_hbm, ug_hbm, dg_hbm,
-           send, recv, xs, ds, act, dgate, dup, scr_a, scr_b, own, other, part, ret,
+def route(x, z, y, cap, swap, slot_cap, ids, gates, itab, ftab, kept_at):
+    tokens = ids.shape[0]
+    count = 2 * tokens
+    experts = slot_cap.shape[0] * slot_cap.shape[1]
+    per, holders = slot_cap.shape[1], slot_cap.shape[0]
+    lane_e = lax.broadcasted_iota(jnp.int32, (1, experts), 1)
+    cap_row = jnp.zeros((1, experts), jnp.int32)
+    for e in range(experts):
+        home, s = e // per, e % per
+        away = (home + holders // 2) % holders
+        cap_e = jnp.where(swap[home % (holders // 2)] == s, slot_cap[away, s], slot_cap[home, s])
+        cap_row = jnp.where(lane_e == e, cap_e, cap_row)
+    ids_c = jnp.concatenate([ids[:, 0:1], ids[:, 1:2]], axis=0)
+    gate_c = jnp.concatenate([gates[:, 0:1], gates[:, 1:2]], axis=0)
+    at_c = lax.broadcasted_iota(jnp.int32, (count, 1), 0)
+    at_r = lax.broadcasted_iota(jnp.int32, (1, count), 1)
+    second_c, second_r = (at_c >= tokens).astype(jnp.int32), (at_r >= tokens).astype(jnp.int32)
+    token_c = at_c - tokens * second_c
+    key_c = 2 * token_c + second_c
+    key_r = 2 * (at_r - tokens * second_r) + second_r
+    same = at_c == at_r
+    ids_r = jnp.sum(jnp.where(same, ids_c, 0), axis=0, keepdims=True)
+    earlier = (ids_c == ids_r) & (key_r < key_c)
+    rank = jnp.sum(earlier.astype(jnp.int32), axis=1, keepdims=True)
+    room = jnp.sum(jnp.where(ids_c == lane_e, cap_row, 0), axis=1, keepdims=True)
+    kept = (rank < room).astype(F32)
+    kx = ((ids_c >> 4) + (SIDE - x)) & 3
+    kz = (((ids_c >> 2) & 3) + (SIDE - z)) & 3
+    ky = ((ids_c & 3) + (SIDE - y)) & 3
+    slot = ((ky + 2 * SIDE - kx - kz) & 3) * 16 + kx * 4 + kz
+    gate_c = gate_c * kept
+    rank = jnp.minimum(rank, cap - 1)
+    match = slot * cap + rank == at_r
+    itab[...] = jnp.zeros_like(itab)
+    ftab[...] = jnp.zeros_like(ftab)
+    itab[0:1, 0:count] = jnp.minimum(jnp.sum(jnp.where(match, token_c, 0), axis=0, keepdims=True), tokens - 1)
+    itab[1:2, 0:count] = jnp.sum(jnp.where(same, slot * 2 * cap + rank, 0), axis=0, keepdims=True)
+    ftab[0:1, 0:count] = jnp.sum(jnp.where(match, gate_c, 0.0), axis=0, keepdims=True)
+    ftab[1:2, 0:count] = jnp.sum(jnp.where(same, gate_c, 0.0), axis=0, keepdims=True)
+    kept_at[...] = kept
+
+
+def kernel(groups, cap, swap, slot_cap, ids, gates, tok, grad, wg_hbm, wu_hbm, wd_hbm,
+           lo, gt, routing, gg_hbm, ug_hbm, dg_hbm,
+           itab, ftab, itab_s, ftab_s, kept_at, inner, tok3, grad3, send, recv, xs, ds, act, dgate, dup, scr_a, scr_b, own, other, part, ret,
            wg, wu, wd, act_t, dgate_t, dup_t, stage,
-           send_sem, recv_sem, fwd_ssem, fwd_rsem, part_ssem, part_rsem, ret_ssem, ret_rsem, w_sem, out_sem):
+           send_sem, recv_sem, fwd_ssem, fwd_rsem, part_ssem, part_rsem, ret_ssem, ret_rsem, w_sem, out_sem, tab_sem):
     width = wg.shape[1]
     units = wg.shape[0]
     cols = width // LANES
     tokens = tok.shape[0]
+    assigns = 2 * tokens
     slots = CHIPS // groups
     half = slots * cap
     rows = 2 * half
@@ -70,12 +113,28 @@
             src_ref=send.at[n], dst_ref=recv.at[0, n], send_sem=send_sem.at[n], recv_sem=recv_sem.at[n],
             device_id=chip(n, 1), device_id_type=MESH)
 
+    route(x, z, y, cap, swap, slot_cap, ids, gates, itab, ftab, kept_at)
+    tables = [
+        pltpu.make_async_copy(itab, itab_s, tab_sem.at[0]),
+        pltpu.make_async_copy(ftab, ftab_s, tab_sem.at[1]),
+    ]
+    for copy in tables:
+        copy.start()
+    for j in range(cols):
+        lanes = slice(j * LANES, (j + 1) * LANES)
+        scr_a[pl.ds(j, tokens, stride=cols), :] = tok[:, lanes].astype(F32)
+        scr_b[pl.ds(j, tokens, stride=cols), :] = grad[:, lanes].astype(F32)
+    tok3[...] = scr_a[pl.ds(0, tokens * cols), :].astype(BF).reshape(tokens, cols, LANES)
+    grad3[...] = scr_b[pl.ds(0, tokens * cols), :].reshape(tokens, cols, LANES)
+    for copy in tables:
+        copy.wait()
+
     def gather(n, put):
         for r in range(cap):
             q = n * cap + r
-            t = idx[q]
-            put(r, tok[t])
-            put(cap + r, (gate_q[q] * grad[t].astype(F32)).astype(BF))
+            t = itab_s[0, q]
+            put(r, tok3[t])
+            put(cap + r, (ftab_s[0, q] * grad3[t]).astype(BF))
 
     def put_own(r, value):
         recv[0, 0, r] = value
@@ -120,11 +179,9 @@
     def compute(g):
         base = g * rows
         first = g * slots
-        forward(g).wait_recv()
-        if g == 0:
-            for i in range(3):
-                weight_copy(i).wait()
         for p in range(2):
+            if p == 1:
+                forward(g).wait_recv()
             def spread(i, _):
                 n0 = first + i * 16
                 r0 = pl.multiple_of(base + p * half + i * 16 * cap, 16)
@@ -136,6 +193,9 @@
                             pl.ds(j, 16 * cap, stride=cols), :].astype(BF)
                 return 0
             lax.fori_loop(0, slots // 16, spread, 0)
+        if g == 0:
+            for i in range(3):
+                weight_copy(i).wait()
         here = pl.ds(base, rows)
 
         def hidden(n, _):
@@ -186,15 +246,13 @@
             ret[0] = (own[0].astype(F32) + part[0].astype(F32)).astype(BF)
         lax.fori_loop(max(g * slots, 1), (g + 1) * slots, one, 0)
 
-    for step in range(groups + 2):
-        if step < groups:
-            arrive(step)
-        if 1 <= step <= groups:
-            compute(step - 1)
-        if step >= 2:
-            finish(step - 2)
-
+    for step in range(groups):
+        arrive(step)
+        if step >= 1:
+            finish(step - 1)
+        compute(step)
     act_t[...] = act[...].T
+    finish(groups - 1)
     dgate_t[...] = dgate[...].T
     dup_t[...] = dup[...].T
     tile = stage.shape[3]
@@ -222,23 +280,30 @@
     lax.fori_loop(1, CHIPS, drain, 0)
 
     def combine(t, _):
-        cot = grad[t].astype(F32)
+        cot = grad3[t]
         total = jnp.zeros((cols, LANES), F32)
         back = jnp.zeros((cols, LANES), F32)
         for k in range(2):
-            a = 2 * t + k
-            q = row_of[a]
+            a = k * tokens + t
+            q = itab_s[1, a]
             n = q // (2 * cap)
             r = q % (2 * cap)
             out_row = ret[n, r].astype(F32)
-            total = total + gate_a[a] * out_row
+            total = total + ftab_s[1, a] * out_row
             back = back + ret[n, r + cap].astype(F32)
-            gr[pl.ds(a, 1), :] = jnp.sum(cot * out_row, axis=0, keepdims=True)
-        lo[t] = total.astype(BF)
-        gt[t] = back.astype(BF)
+            inner[pl.ds(a, 1), :] = jnp.sum(cot * out_row, axis=0, keepdims=True)
+        at = pl.ds(pl.multiple_of(t * cols, cols), cols)
+        scr_a[at, :] = total
+        scr_b[at, :] = back
         return 0
 
-    lax.fori_loop(0, tokens, combine, 0)
+    lax.fori_loop(0, tokens, combine, 0, unroll=8)
+    for j in range(cols):
+        lanes = slice(j * LANES, (j + 1) * LANES)
+        lo[:, lanes] = scr_a[pl.ds(j, tokens, stride=cols), :].astype(BF)
+        gt[:, lanes] = scr_b[pl.ds(j, tokens, stride=cols), :].astype(BF)
+    product = jnp.where(kept_at[...] > 0.0, jnp.sum(inner[...], axis=1, keepdims=True), 0.0)
+    routing[...] = jnp.concatenate([product[:tokens], product[tokens:]], axis=1)
 
     def settle(n, _):
         dispatch(n).wait_send()
@@ -263,48 +328,32 @@
     cap = count * top // experts
     assigns = count * top
     cols = width // LANES
-    groups = 2
+    groups = 4
     slots = CHIPS // groups
     rows = 2 * slots * cap
-
-    h = lax.axis_index("expert")
-    d = lax.axis_index("dp")
-    half = holders // 2
-    moved = jnp.concatenate([swap_slot, swap_slot])[:, None] == jnp.arange(per, dtype=jnp.int32)[None, :]
-    rolled = jnp.concatenate([slot_cap[half:], slot_cap[:half]], axis=0)
-    capacity = jnp.where(moved, rolled, slot_cap).reshape(experts)
-    ids = expert_ids.reshape(-1)
-    gates = gate_weights.reshape(-1)
-    a_range = jnp.arange(assigns, dtype=jnp.int32)
-    rank = jnp.sum(((ids[:, None] == ids[None, :]) & (a_range[None, :] < a_range[:, None])).astype(jnp.int32), axis=1)
-    my_cap = jnp.sum(
-        jnp.where(ids[:, None] == jnp.arange(experts, dtype=jnp.int32)[None, :], capacity[None, :], 0), axis=1)
-    kept = rank < my_cap
-    kx = (ids // 16 + SIDE - h // SIDE) % SIDE
-    kz = ((ids // 4) % 4 + SIDE - h % SIDE) % SIDE
-    ky = (ids % 4 + SIDE - d // 2) % SIDE
-    slot = ((ky + 2 * SIDE - kx - kz) % SIDE) * 16 + kx * 4 + kz
-    position = slot * cap + rank
-    row_of = slot * 2 * cap + rank
-    gate_a = jnp.where(kept, gates, 0.0)
-    match = position[None, :] == a_range[:, None]
-    idx = jnp.sum(jnp.where(match, (a_range // top)[None, :], 0), axis=1)
-    gate_q = jnp.sum(jnp.where(match, gate_a[None, :], 0.0), axis=1)
 
     smem = pl.BlockSpec(memory_space=pltpu.SMEM)
     vmem = pl.BlockSpec(memory_space=pltpu.VMEM)
     hbm = pl.BlockSpec(memory_space=pl.ANY)
-    rows3 = jax.ShapeDtypeStruct((count, cols, LANES), BF)
+    flat_rows = jax.ShapeDtypeStruct((count, width), BF)
     block = (CHIPS, 2 * cap, cols, LANES)
     total = 2 * CHIPS * cap
     weights = jax.ShapeDtypeStruct((1, units, width), BF)
     dma = pltpu.SemaphoreType.DMA
-    lo, gt, gr, gg, ug, dg = pl.pallas_call(
+    return pl.pallas_call(
         functools.partial(kernel, groups, cap),
-        out_shape=(rows3, rows3, jax.ShapeDtypeStruct((assigns, LANES), F32), weights, weights, weights),
-        in_specs=[smem] * 4 + [vmem] * 2 + [hbm] * 3,
+        out_shape=(flat_rows, flat_rows, jax.ShapeDtypeStruct((count, top), F32), weights, weights, weights),
+        in_specs=[smem] * 2 + [vmem] * 4 + [hbm] * 3,
         out_specs=(vmem, vmem, vmem, hbm, hbm, hbm),
         scratch_shapes=[
+            pltpu.VMEM((8, 384), jnp.int32),
+            pltpu.VMEM((8, 384), F32),
+            pltpu.SMEM((8, 384), jnp.int32),
+            pltpu.SMEM((8, 384), F32),
+            pltpu.VMEM((assigns, 1), F32),
+            pltpu.VMEM((assigns, LANES), F32),
+            pltpu.VMEM((count, cols, LANES), BF),
+            pltpu.VMEM((count, cols, LANES), F32),
             pltpu.VMEM(block, BF),
             pltpu.VMEM((2,) + block, BF),
             pltpu.VMEM((total, width), BF),
@@ -335,15 +384,13 @@
             dma((CHIPS,)),
             dma((3,)),
             dma((2, 3)),
+            dma((2,)),
         ],
         compiler_params=pltpu.CompilerParams(
             collective_id=0, has_side_effects=True, vmem_limit_bytes=62 * 1024 * 1024),
         cost_estimate=pl.CostEstimate(
             flops=18 * total * units * width, bytes_accessed=12 * units * width, transcendentals=0),
-    )(idx, gate_q, row_of, gate_a, tokens.reshape(count, cols, LANES), grad_output.reshape(count, cols, LANES),
-      gate_weight, up_weight, down_weight)
-    routing = jnp.where(kept, jnp.sum(gr, axis=1), 0.0).reshape(count, top)
-    return lo.reshape(count, width), gt.reshape(count, width), routing, gg, ug, dg
+    )(swap_slot, slot_cap, expert_ids, gate_weights, tokens, grad_output, gate_weight, up_weight, down_weight)
 
 
 def solution(mesh):

time: 135 us -> 114 us (0.84)
  Pallas kernels: 108 us -> 94.4 us
  other arithmetic: 5.05 us -> 0 us
  local copies, waits for them, and re-layouts: 20.8 us -> 18.5 us
    pallas_call x1, Pallas kernels: 108 us -> 94.4 us  [body(): pl.pallas_call(functools.partial(kernel, groups, cap), out_shape=(flat_ro...]
    reduce_sum x5 -> x0, other arithmetic: 2.84 us -> none  [the longest x1 1.06 us: body(): routing = jnp.where(kept, jnp.sum(gr, axis=1), 0.0).reshape(count, top)]
    unnamed x16 -> x12, local copies, waits for them, and re-layouts: 19.4 us -> 17 us
    pallas_call x0 -> x1, local copies, waits for them, and re-layouts: none -> 1.54 us  [body(): pl.pallas_call(functools.partial(kernel, groups, cap), out_shape=(flat_ro...]
where the time goes in v1:
time: 114 us
  Pallas kernels  94.4 us (83%)
  local copies, waits for them, and re-layouts  18.5 us (16%)
    pallas_call x1, Pallas kernels, body(): pl.pallas_call(functools.partial(kernel, groups, cap), out_shape=(flat_ro...  94.4 us
    unnamed x12, local copies, waits for them, and re-layouts  17 us

profile of v1, /device:TPU:1, one launch (start us, length us, event | category | flops | bytes accessed | tf_op | source)
XLA Modules:
  0.0 113.6 jit_solution(14341717346892068087)
XLA Ops:
  0.6 1.4 %copy.15.slot_cap = s32[16,4]{1,0:T(8,128)} copy(s32[16,4]{0,1:T(4,128)} %param.17) | data formatting | bytes 512 | tf_op args[8]
  2.0 1.4 %copy.16.ids = s32[160,2]{1,0:T(8,128)} copy(s32[160,2]{0,1:T(2,128)} %param.10) | data formatting | bytes 2560 | tf_op args[1]
  3.4 1.4 %copy.17.gates = f32[160,2]{1,0:T(8,128)} copy(f32[160,2]{0,1:T(2,128)} %param.11) | data formatting | bytes 2560 | tf_op args[2]
  4.8 94.4 %shard_map.136 = (bf16[160,2048]{1,0:T(8,128)(2,1)}, bf16[160,2048]{1,0:T(8,128)(2,1)}, f32[160,2]{1,0:T(8,128)}, bf16[1,768,2048]{2,1,0:T(8,128)(2,1)}, bf16[1,...) custom-call(s32[8]{0:T(128)} %swap.1, s32[16,4]{1,0:T(8,128)} %copy.15.slot_cap, s32[160,2]{1,0:T(8,128)} %copy.16.ids, ...), custom_call_target="tpu_custom_call" | custom-call | flops 18119393280 | bytes 18874368 | tf_op jit(solution)/shard_map/pallas_call | solution.py:343
  99.2 1.5 %copy.18 = f32[160,2]{0,1:T(2,128)} copy(f32[160,2]{1,0:T(8,128)} %get-tuple-element.8) | data formatting | bytes 2560 | tf_op jit(solution)/shard_map/pallas_call | solution.py:343
  100.8 2.0 %copy.24 = bf16[160,2048]{1,0:T(8,128)(2,1)} copy(bf16[160,2048]{1,0:T(8,128)(2,1)} %get-tuple-element.18) | data formatting | bytes 1310720
  102.8 2.0 %copy.25 = bf16[160,2048]{1,0:T(8,128)(2,1)} copy(bf16[160,2048]{1,0:T(8,128)(2,1)} %get-tuple-element.19) | data formatting | bytes 1310720
  104.7 0.0 copy-start.1
  104.7 4.1 %copy.26 = bf16[1,768,2048]{2,1,0:T(8,128)(2,1)} copy(bf16[1,768,2048]{2,1,0:T(8,128)(2,1)} %get-tuple-element.21) | data formatting | bytes 6291456
  108.9 0.0 copy-done.1
  108.9 0.0 copy-start
  108.9 1.7 %copy.27 = bf16[1,768,2048]{2,1,0:T(8,128)(2,1)} copy(bf16[1,768,2048]{2,1,0:T(8,128)(2,1)S(1)} %copy-done.1) | data formatting | bytes 6291456
  110.5 1.4 %copy-done = bf16[1,768,2048]{2,1,0:T(8,128)(2,1)S(1)} copy-done((bf16[1,768,2048]{2,1,0:T(8,128)(2,1)S(1)}, bf16[1,768,2048]{2,1,0:T(8,128)(2,1)}, u32[]{:S(2)}) %copy-start) | copy-done | bytes 3145752
  111.9 1.7 %copy.28 = bf16[1,768,2048]{2,1,0:T(8,128)(2,1)} copy(bf16[1,768,2048]{2,1,0:T(8,128)(2,1)S(1)} %copy-done) | data formatting | bytes 6291456
Async XLA Ops:
  104.7 4.1 %copy-start.1 = (bf16[1,768,2048]{2,1,0:T(8,128)(2,1)S(1)}, bf16[1,768,2048]{2,1,0:T(8,128)(2,1)}, u32[]{:S(2)}) copy-start(bf16[1,768,2048]{2,1,0:T(8,128)(2,1)} %get-tuple-element.22) | copy-start | bytes 9437188
  108.9 3.0 %copy-start = (bf16[1,768,2048]{2,1,0:T(8,128)(2,1)S(1)}, bf16[1,768,2048]{2,1,0:T(8,128)(2,1)}, u32[]{:S(2)}) copy-start(bf16[1,768,2048]{2,1,0:T(8,128)(2,1)} %get-tuple-element.23) | copy-start | bytes 9437188

commit v2 on v1

--- a/solution.py
+++ b/solution.py
@@ -26,26 +26,31 @@
     return n1, n0, (n2 + n1 + n0) % 4
 
 
-def route(x, z, y, cap, swap, slot_cap, ids, gates, itab, ftab, kept_at):
-    tokens = ids.shape[0]
+def route(x, z, y, cap, swap, slot_cap, ids, gates, itab, ftab):
+    tokens = ids.shape[1]
     count = 2 * tokens
-    experts = slot_cap.shape[0] * slot_cap.shape[1]
-    per, holders = slot_cap.shape[1], slot_cap.shape[0]
+    per, holders = slot_cap.shape
+    experts = per * holders
     lane_e = lax.broadcasted_iota(jnp.int32, (1, experts), 1)
     cap_row = jnp.zeros((1, experts), jnp.int32)
     for e in range(experts):
         home, s = e // per, e % per
         away = (home + holders // 2) % holders
-        cap_e = jnp.where(swap[home % (holders // 2)] == s, slot_cap[away, s], slot_cap[home, s])
+        cap_e = jnp.where(swap[home % (holders // 2)] == s, slot_cap[s, away], slot_cap[s, home])
         cap_row = jnp.where(lane_e == e, cap_e, cap_row)
-    ids_c = jnp.concatenate([ids[:, 0:1], ids[:, 1:2]], axis=0)
-    gate_c = jnp.concatenate([gates[:, 0:1], gates[:, 1:2]], axis=0)
     at_c = lax.broadcasted_iota(jnp.int32, (count, 1), 0)
     at_r = lax.broadcasted_iota(jnp.int32, (1, count), 1)
     second_c, second_r = (at_c >= tokens).astype(jnp.int32), (at_r >= tokens).astype(jnp.int32)
     token_c = at_c - tokens * second_c
     key_c = 2 * token_c + second_c
     key_r = 2 * (at_r - tokens * second_r) + second_r
+    mine = token_c == lax.broadcasted_iota(jnp.int32, (1, tokens), 1)
+
+    def column(ref):
+        value = jnp.where(second_c == 1, ref[1:2, :], ref[0:1, :])
+        return jnp.sum(jnp.where(mine, value, jnp.zeros_like(value)), axis=1, keepdims=True)
+
+    ids_c, gate_c = column(ids), column(gates)
     same = at_c == at_r
     ids_r = jnp.sum(jnp.where(same, ids_c, 0), axis=0, keepdims=True)
     earlier = (ids_c == ids_r) & (key_r < key_c)
@@ -65,19 +70,32 @@
     itab[1:2, 0:count] = jnp.sum(jnp.where(same, slot * 2 * cap + rank, 0), axis=0, keepdims=True)
     ftab[0:1, 0:count] = jnp.sum(jnp.where(match, gate_c, 0.0), axis=0, keepdims=True)
     ftab[1:2, 0:count] = jnp.sum(jnp.where(same, gate_c, 0.0), axis=0, keepdims=True)
-    kept_at[...] = kept
+    ftab[2:3, 0:count] = jnp.sum(jnp.where(same, kept, 0.0), axis=0, keepdims=True)
+
+
+def turning():
+    row = lax.broadcasted_iota(jnp.int32, (256, 256), 0)
+    column = lax.broadcasted_iota(jnp.int32, (256, 256), 1)
+    return (((row & 15) << 4) + (row >> 4) == column).astype(F32).astype(BF)
+
+
+def to_tiles(turn, left, right, rows):
+    parts = []
+    for j in range(16):
+        lanes = slice(j * LANES, (j + 1) * LANES)
+        parts.append(jnp.concatenate([left[rows, lanes], right[rows, lanes]], axis=1))
+    return dot(turn[...], jnp.concatenate(parts, axis=0), NN)
 
 
 def kernel(groups, cap, swap, slot_cap, ids, gates, tok, grad, wg_hbm, wu_hbm, wd_hbm,
-           lo, gt, routing, gg_hbm, ug_hbm, dg_hbm,
-           itab, ftab, itab_s, ftab_s, kept_at, inner, tok3, grad3, send, recv, xs, ds, act, dgate, dup, scr_a, scr_b, own, other, part, ret,
+           ret, itab, ftab, gg_hbm, ug_hbm, dg_hbm,
+           itab_s, ftab_s, turn, tok3, grad3, send, recv, xs, ds, act, dgate, dup, ys, dxs, own, other, part,
            wg, wu, wd, act_t, dgate_t, dup_t, stage,
            send_sem, recv_sem, fwd_ssem, fwd_rsem, part_ssem, part_rsem, ret_ssem, ret_rsem, w_sem, out_sem, tab_sem):
     width = wg.shape[1]
     units = wg.shape[0]
     cols = width // LANES
     tokens = tok.shape[0]
-    assigns = 2 * tokens
     slots = CHIPS // groups
     half = slots * cap
     rows = 2 * half
@@ -113,19 +131,19 @@
             src_ref=send.at[n], dst_ref=recv.at[0, n], send_sem=send_sem.at[n], recv_sem=recv_sem.at[n],
             device_id=chip(n, 1), device_id_type=MESH)
 
-    route(x, z, y, cap, swap, slot_cap, ids, gates, itab, ftab, kept_at)
+    route(x, z, y, cap, swap, slot_cap, ids, gates, itab, ftab)
     tables = [
         pltpu.make_async_copy(itab, itab_s, tab_sem.at[0]),
         pltpu.make_async_copy(ftab, ftab_s, tab_sem.at[1]),
     ]
     for copy in tables:
         copy.start()
-    for j in range(cols):
-        lanes = slice(j * LANES, (j + 1) * LANES)
-        scr_a[pl.ds(j, tokens, stride=cols), :] = tok[:, lanes].astype(F32)
-        scr_b[pl.ds(j, tokens, stride=cols), :] = grad[:, lanes].astype(F32)
-    tok3[...] = scr_a[pl.ds(0, tokens * cols), :].astype(BF).reshape(tokens, cols, LANES)
-    grad3[...] = scr_b[pl.ds(0, tokens * cols), :].reshape(tokens, cols, LANES)
+    turn[...] = turning()
+    for b in range(tokens // 16):
+        at = slice(b * 16, (b + 1) * 16)
+        tiles = to_tiles(turn, tok, grad, at)
+        tok3[at] = tiles[:, :LANES].astype(BF).reshape(16, cols, LANES)
+        grad3[at] = tiles[:, LANES:].reshape(16, cols, LANES)
     for copy in tables:
         copy.wait()
 
@@ -168,6 +186,8 @@
         return pltpu.make_async_remote_copy(
             src_ref=own.at[n], dst_ref=ret.at[n], send_sem=ret_ssem.at[n], recv_sem=ret_rsem.at[n],
             device_id=chip(n, -1), device_id_type=MESH)
+
+    keep = pltpu.make_async_copy(own.at[0], ret.at[0], tab_sem.at[2])
 
     def arrive(g):
         def one(n, _):
@@ -183,14 +203,19 @@
             if p == 1:
                 forward(g).wait_recv()
             def spread(i, _):
-                n0 = first + i * 16
-                r0 = pl.multiple_of(base + p * half + i * 16 * cap, 16)
-                for lo_row, scr, dst in ((0, scr_a, xs), (cap, scr_b, ds)):
-                    value = recv[p, pl.ds(n0, 16), lo_row:lo_row + cap].astype(F32)
-                    scr[pl.ds(0, 16 * cap * cols), :] = value.reshape(16 * cap * cols, LANES)
+                r0 = base + p * half + i * 16 * cap
+                value = recv[p, pl.ds(first + i * 16, 16)]
+                left = value[:, :cap].reshape(16 * cap * cols, LANES)
+                right = value[:, cap:].reshape(16 * cap * cols, LANES)
+                for b in range(cap):
+                    at = slice(b * 256, (b + 1) * 256)
+                    pair = jnp.concatenate([left[at], right[at]], axis=1)
+                    turned = dot(turn[...], pair, NN).astype(BF)
+                    here = pl.ds(pl.multiple_of(r0 + b * 16, 16), 16)
                     for j in range(cols):
-                        dst[pl.ds(r0, 16 * cap), j * LANES:(j + 1) * LANES] = scr[
-                            pl.ds(j, 16 * cap, stride=cols), :].astype(BF)
+                        lanes = slice(j * LANES, (j + 1) * LANES)
+                        xs[here, lanes] = turned[j * 16:(j + 1) * 16, :LANES]
+                        ds[here, lanes] = turned[j * 16:(j + 1) * 16, LANES:]
                 return 0
             lax.fori_loop(0, slots // 16, spread, 0)
         if g == 0:
@@ -216,19 +241,21 @@
             f = pl.ds(pl.multiple_of(n * 256, 256), 256)
             out = dot(act[here, :], wd[:, f], NN)
             back = dot(dgate[here, :], wg[:, f], NN) + dot(dup[here, :], wu[:, f], NN)
-            for k in range(2):
-                lanes = slice(k * LANES, (k + 1) * LANES)
-                scr_a[pl.ds(n * 2 + k, rows, stride=cols), :] = out[:, lanes]
-                scr_b[pl.ds(n * 2 + k, rows, stride=cols), :] = back[:, lanes]
+            ys[:, f] = out.astype(BF)
+            dxs[:, f] = back.astype(BF)
             return 0
 
         lax.fori_loop(0, width // 256, model, 0)
         for p, dst in ((0, own), (1, other)):
             def pack(i, _):
                 n0 = first + i * 16
-                at = pl.ds(pl.multiple_of((p * half + i * 16 * cap) * cols, 16), 16 * cap * cols)
-                for lo_row, scr in ((0, scr_a), (cap, scr_b)):
-                    dst[pl.ds(n0, 16), lo_row:lo_row + cap] = scr[at, :].astype(BF).reshape(16, cap, cols, LANES)
+                r0 = p * half + i * 16 * cap
+                tiles = [
+                    to_tiles(turn, ys, dxs, pl.ds(pl.multiple_of(r0 + b * 16, 16), 16)).astype(BF) for b in range(cap)]
+                for k in range(2):
+                    lanes = slice(k * LANES, (k + 1) * LANES)
+                    rows3 = jnp.concatenate([t[:, lanes] for t in tiles], axis=0)
+                    dst[pl.ds(n0, 16), k * cap:(k + 1) * cap] = rows3.reshape(16, cap, cols, LANES)
                 return 0
             lax.fori_loop(0, slots // 16, pack, 0)
         trade(g).start()
@@ -237,13 +264,13 @@
         trade(g).wait_recv()
 
         def one(n, _):
-            total = (own[n].astype(F32) + part[n].astype(F32)).astype(BF)
-            own[n] = total
+            own[n] = (own[n].astype(F32) + part[n].astype(F32)).astype(BF)
             give_back(n).start()
             return 0
 
         if g == 0:
-            ret[0] = (own[0].astype(F32) + part[0].astype(F32)).astype(BF)
+            own[0] = (own[0].astype(F32) + part[0].astype(F32)).astype(BF)
+            keep.start()
         lax.fori_loop(max(g * slots, 1), (g + 1) * slots, one, 0)
 
     for step in range(groups):
@@ -278,6 +305,48 @@
         return 0
 
     lax.fori_loop(1, CHIPS, drain, 0)
+
+    keep.wait()
+
+    def settle(n, _):
+        dispatch(n).wait_send()
+        give_back(n).wait_send()
+        return 0
+
+    lax.fori_loop(1, CHIPS, settle, 0)
+    for g in range(groups):
+        forward(g).wait_send()
+        trade(g).wait_send()
+    for n in range(max(steps - 2, 0), steps):
+        for i in range(3):
+            out_copy(i, n % 2, n).wait()
+
+
+def last_kernel(cap, pieces, grad, itab, ftab, ret_hbm, gg_in, ug_in, dg_in,
+                lo, gt, routing, gg, ug, dg,
+                itab_s, ftab_s, ret, turn, grad3, total3, back3, inner, tab_sem, ret_sem, out_sem):
+    tokens, width = grad.shape
+    cols = width // LANES
+    rows = gg.shape[1] // pieces
+    fetch = [pltpu.make_async_copy(itab, itab_s, tab_sem.at[0]), pltpu.make_async_copy(ftab, ftab_s, tab_sem.at[1]),
+             pltpu.make_async_copy(ret_hbm, ret, ret_sem)]
+    moves = [
+        pltpu.make_async_copy(src.at[0, pl.ds(k * rows, rows)], dst.at[0, pl.ds(k * rows, rows)], out_sem.at[i, k])
+        for i, (src, dst) in enumerate(((gg_in, gg), (ug_in, ug), (dg_in, dg))) for k in range(pieces)]
+    for copy in fetch + moves:
+        copy.start()
+    turn[...] = turning()
+    for b in range(tokens // 32):
+        low, high = slice(b * 32, b * 32 + 16), slice(b * 32 + 16, b * 32 + 32)
+        parts = []
+        for j in range(cols):
+            lanes = slice(j * LANES, (j + 1) * LANES)
+            parts.append(jnp.concatenate([grad[low, lanes], grad[high, lanes]], axis=1))
+        tiles = dot(turn[...], jnp.concatenate(parts, axis=0), NN)
+        grad3[low] = tiles[:, :LANES].reshape(16, cols, LANES)
+        grad3[high] = tiles[:, LANES:].reshape(16, cols, LANES)
+    for copy in fetch:
+        copy.wait()
 
     def combine(t, _):
         cot = grad3[t]
@@ -291,32 +360,28 @@
             out_row = ret[n, r].astype(F32)
             total = total + ftab_s[1, a] * out_row
             back = back + ret[n, r + cap].astype(F32)
-            inner[pl.ds(a, 1), :] = jnp.sum(cot * out_row, axis=0, keepdims=True)
-        at = pl.ds(pl.multiple_of(t * cols, cols), cols)
-        scr_a[at, :] = total
-        scr_b[at, :] = back
+            product = jnp.sum(cot * out_row, axis=0, keepdims=True)
+            inner[pl.ds(a, 1), :] = jnp.where(ftab_s[2, a] > 0.0, product, 0.0)
+        total3[t] = total.astype(BF)
+        back3[t] = back.astype(BF)
         return 0
 
     lax.fori_loop(0, tokens, combine, 0, unroll=8)
-    for j in range(cols):
-        lanes = slice(j * LANES, (j + 1) * LANES)
-        lo[:, lanes] = scr_a[pl.ds(j, tokens, stride=cols), :].astype(BF)
-        gt[:, lanes] = scr_b[pl.ds(j, tokens, stride=cols), :].astype(BF)
-    product = jnp.where(kept_at[...] > 0.0, jnp.sum(inner[...], axis=1, keepdims=True), 0.0)
-    routing[...] = jnp.concatenate([product[:tokens], product[tokens:]], axis=1)
-
-    def settle(n, _):
-        dispatch(n).wait_send()
-        give_back(n).wait_send()
-        return 0
-
-    lax.fori_loop(1, CHIPS, settle, 0)
-    for g in range(groups):
-        forward(g).wait_send()
-        trade(g).wait_send()
-    for n in range(max(steps - 2, 0), steps):
-        for i in range(3):
-            out_copy(i, n % 2, n).wait()
+    for b in range(tokens // 16):
+        at = slice(b * 16, (b + 1) * 16)
+        pair = jnp.concatenate([total3[at].reshape(256, LANES), back3[at].reshape(256, LANES)], axis=1)
+        turned = dot(turn[...], pair, NN).astype(BF)
+        for j in range(cols):
+            lanes = slice(j * LANES, (j + 1) * LANES)
+            lo[at, lanes] = turned[j * 16:(j + 1) * 16, :LANES]
+            gt[at, lanes] = turned[j * 16:(j + 1) * 16, LANES:]
+    sums = jnp.sum(inner[...], axis=1, keepdims=True)
+    spot = lax.broadcasted_iota(jnp.int32, (tokens, tokens), 0) == lax.broadcasted_iota(jnp.int32, (tokens, tokens), 1)
+    for k in range(2):
+        routing[k:k + 1, :] = jnp.sum(
+            jnp.where(spot, sums[k * tokens:(k + 1) * tokens], 0.0), axis=0, keepdims=True)
+    for copy in moves:
+        copy.wait()
 
 
 def body(tokens, expert_ids, gate_weights, grad_output, gate_weight, up_weight, down_weight, swap_slot, slot_cap):
@@ -328,7 +393,8 @@
     cap = count * top // experts
     assigns = count * top
     cols = width // LANES
-    groups = 4
+    groups = 2
+    pieces = 4
     slots = CHIPS // groups
     rows = 2 * slots * cap
 
@@ -340,18 +406,16 @@
     total = 2 * CHIPS * cap
     weights = jax.ShapeDtypeStruct((1, units, width), BF)
     dma = pltpu.SemaphoreType.DMA
-    return pl.pallas_call(
+    ret, itab, ftab, *grads = pl.pallas_call(
         functools.partial(kernel, groups, cap),
-        out_shape=(flat_rows, flat_rows, jax.ShapeDtypeStruct((count, top), F32), weights, weights, weights),
+        out_shape=(jax.ShapeDtypeStruct(block, BF), jax.ShapeDtypeStruct((8, 384), jnp.int32),
+                   jax.ShapeDtypeStruct((8, 384), F32), weights, weights, weights),
         in_specs=[smem] * 2 + [vmem] * 4 + [hbm] * 3,
-        out_specs=(vmem, vmem, vmem, hbm, hbm, hbm),
+        out_specs=(hbm, vmem, vmem, hbm, hbm, hbm),
         scratch_shapes=[
-            pltpu.VMEM((8, 384), jnp.int32),
-            pltpu.VMEM((8, 384), F32),
             pltpu.SMEM((8, 384), jnp.int32),
             pltpu.SMEM((8, 384), F32),
-            pltpu.VMEM((assigns, 1), F32),
-            pltpu.VMEM((assigns, LANES), F32),
+            pltpu.VMEM((256, 256), BF),
             pltpu.VMEM((count, cols, LANES), BF),
             pltpu.VMEM((count, cols, LANES), F32),
             pltpu.VMEM(block, BF),
@@ -361,9 +425,8 @@
             pltpu.VMEM((total, units), BF),
             pltpu.VMEM((total, units), BF),
             pltpu.VMEM((total, units), BF),
-            pltpu.VMEM((rows * cols, LANES), F32),
-            pltpu.VMEM((rows * cols, LANES), F32),
-            pltpu.VMEM(block, BF),
+            pltpu.VMEM((rows, width), BF),
+            pltpu.VMEM((rows, width), BF),
             pltpu.VMEM(block, BF),
             pltpu.VMEM(block, BF),
             pltpu.VMEM(block, BF),
@@ -384,13 +447,35 @@
             dma((CHIPS,)),
             dma((3,)),
             dma((2, 3)),
-            dma((2,)),
+            dma((3,)),
         ],
         compiler_params=pltpu.CompilerParams(
             collective_id=0, has_side_effects=True, vmem_limit_bytes=62 * 1024 * 1024),
         cost_estimate=pl.CostEstimate(
             flops=18 * total * units * width, bytes_accessed=12 * units * width, transcendentals=0),
-    )(swap_slot, slot_cap, expert_ids, gate_weights, tokens, grad_output, gate_weight, up_weight, down_weight)
+    )(swap_slot, slot_cap.T, expert_ids.T, gate_weights.T, tokens, grad_output, gate_weight, up_weight, down_weight)
+    lo, gt, routing, gg, ug, dg = pl.pallas_call(
+        functools.partial(last_kernel, cap, pieces),
+        out_shape=(flat_rows, flat_rows, jax.ShapeDtypeStruct((top, count), F32), weights, weights, weights),
+        in_specs=[vmem] * 3 + [hbm] * 4,
+        out_specs=(vmem, vmem, vmem, hbm, hbm, hbm),
+        scratch_shapes=[
+            pltpu.SMEM((8, 384), jnp.int32),
+            pltpu.SMEM((8, 384), F32),
+            pltpu.VMEM(block, BF),
+            pltpu.VMEM((256, 256), BF),
+            pltpu.VMEM((count, cols, LANES), F32),
+            pltpu.VMEM((count, cols, LANES), BF),
+            pltpu.VMEM((count, cols, LANES), BF),
+            pltpu.VMEM((assigns, LANES), F32),
+            dma((2,)),
+            dma,
+            dma((3, pieces)),
+        ],
+        compiler_params=pltpu.CompilerParams(vmem_limit_bytes=62 * 1024 * 1024),
+        cost_estimate=pl.CostEstimate(flops=0, bytes_accessed=12 * units * width, transcendentals=0),
+    )(grad_output, itab, ftab, ret, *grads)
+    return lo, gt, routing.T, gg, ug, dg
 
 
 def solution(mesh):

time: 114 us -> 377 us (3.31)
  Pallas kernels: 94.4 us -> 376 us
  local copies, waits for them, and re-layouts: 18.5 us -> 0 us
    pallas_call x1 -> x2, Pallas kernels: 94.4 us -> 376 us  [the longest x1 289 us: body(): pl.pallas_call(functools.partial(last_kernel, cap, pieces), out_shape=(fl...]
    unnamed x12 -> x0, local copies, waits for them, and re-layouts: 17 us -> none
where the time goes in v2:
time: 377 us
  Pallas kernels  376 us (100%)
    pallas_call x1, Pallas kernels, body(): pl.pallas_call(functools.partial(last_kernel, cap, pieces), out_shape=(fl...  289 us
    pallas_call x1, Pallas kernels, body(): pl.pallas_call(functools.partial(kernel, groups, cap), out_shape=(jax.Sha...  86.6 us

profile of v2, /device:TPU:1, one launch (start us, length us, event | category | flops | bytes accessed | tf_op | source)
XLA Modules:
  0.0 376.7 jit_solution(18443669258301086926)
XLA Ops:
  0.6 86.6 %shard_map.136 = (bf16[64,10,16,128]{3,2,1,0:T(8,128)(2,1)}, s32[8,384]{1,0:T(8,128)}, f32[8,384]{1,0:T(8,128)}, bf16[1,768,2048]{2,1,0:T(8,128)(2,1)}, bf16[1,7...) custom-call(s32[8]{0:T(128)} %swap.1, s32[4,16]{1,0:T(4,128)} %bitcast.4, s32[2,160]{1,0:T(2,128)} %bitcast.5, ...), custom_call_target="tpu_custom_call" | custom-call | flops 18119393280 | bytes 18874368 | tf_op jit(solution)/shard_map/pallas_call | solution.py:409
  87.2 289.3 %shard_map.137 = (bf16[160,2048]{1,0:T(8,128)(2,1)}, bf16[160,2048]{1,0:T(8,128)(2,1)}, f32[2,160]{1,0:T(2,128)}, bf16[1,768,2048]{2,1,0:T(8,128)(2,1)}, bf16[1,...) custom-call(bf16[160,2048]{1,0:T(8,128)(2,1)} %grad.3, s32[8,384]{1,0:T(8,128)} %get-tuple-element.18.itab, ...), custom_call_target="tpu_custom_call" | custom-call | bytes 18874368 | tf_op jit(solution)/shard_map/pallas_call | solution.py:457

commit v3 on v2

--- a/solution.py
+++ b/solution.py
@@ -70,7 +70,9 @@
     itab[1:2, 0:count] = jnp.sum(jnp.where(same, slot * 2 * cap + rank, 0), axis=0, keepdims=True)
     ftab[0:1, 0:count] = jnp.sum(jnp.where(match, gate_c, 0.0), axis=0, keepdims=True)
     ftab[1:2, 0:count] = jnp.sum(jnp.where(same, gate_c, 0.0), axis=0, keepdims=True)
-    ftab[2:3, 0:count] = jnp.sum(jnp.where(same, kept, 0.0), axis=0, keepdims=True)
+    for k in range(2):
+        ftab[2 + k:3 + k, 0:tokens] = jnp.sum(
+            jnp.where(mine & (second_c == k), kept, 0.0), axis=0, keepdims=True)
 
 
 def turning():
@@ -324,16 +326,19 @@
 
 def last_kernel(cap, pieces, grad, itab, ftab, ret_hbm, gg_in, ug_in, dg_in,
                 lo, gt, routing, gg, ug, dg,
-                itab_s, ftab_s, ret, turn, grad3, total3, back3, inner, tab_sem, ret_sem, out_sem):
+                itab_s, ftab_s, ret, turn, grad3, total3, back3, inner, held, tab_sem, ret_sem, in_sem, out_sem):
     tokens, width = grad.shape
     cols = width // LANES
     rows = gg.shape[1] // pieces
     fetch = [pltpu.make_async_copy(itab, itab_s, tab_sem.at[0]), pltpu.make_async_copy(ftab, ftab_s, tab_sem.at[1]),
              pltpu.make_async_copy(ret_hbm, ret, ret_sem)]
-    moves = [
-        pltpu.make_async_copy(src.at[0, pl.ds(k * rows, rows)], dst.at[0, pl.ds(k * rows, rows)], out_sem.at[i, k])
-        for i, (src, dst) in enumerate(((gg_in, gg), (ug_in, ug), (dg_in, dg))) for k in range(pieces)]
-    for copy in fetch + moves:
+    loads, stores = [], []
+    for i, (src, dst) in enumerate(((gg_in, gg), (ug_in, ug), (dg_in, dg))):
+        for k in range(pieces):
+            at = pl.ds(k * rows, rows)
+            loads.append(pltpu.make_async_copy(src.at[0, at], held.at[i, at], in_sem.at[i, k]))
+            stores.append(pltpu.make_async_copy(held.at[i, at], dst.at[0, at], out_sem.at[i, k]))
+    for copy in fetch + loads:
         copy.start()
     turn[...] = turning()
     for b in range(tokens // 32):
@@ -355,32 +360,34 @@
         for k in range(2):
             a = k * tokens + t
             q = itab_s[1, a]
-            n = q // (2 * cap)
-            r = q % (2 * cap)
-            out_row = ret[n, r].astype(F32)
+            out_row = ret[q].astype(F32)
             total = total + ftab_s[1, a] * out_row
-            back = back + ret[n, r + cap].astype(F32)
-            product = jnp.sum(cot * out_row, axis=0, keepdims=True)
-            inner[pl.ds(a, 1), :] = jnp.where(ftab_s[2, a] > 0.0, product, 0.0)
+            back = back + ret[q + cap].astype(F32)
+            inner[pl.ds(a, 1), :] = jnp.sum(cot * out_row, axis=0, keepdims=True)
         total3[t] = total.astype(BF)
         back3[t] = back.astype(BF)
         return 0
 
-    lax.fori_loop(0, tokens, combine, 0, unroll=8)
-    for b in range(tokens // 16):
-        at = slice(b * 16, (b + 1) * 16)
-        pair = jnp.concatenate([total3[at].reshape(256, LANES), back3[at].reshape(256, LANES)], axis=1)
-        turned = dot(turn[...], pair, NN).astype(BF)
-        for j in range(cols):
-            lanes = slice(j * LANES, (j + 1) * LANES)
-            lo[at, lanes] = turned[j * 16:(j + 1) * 16, :LANES]
-            gt[at, lanes] = turned[j * 16:(j + 1) * 16, LANES:]
+    chunks = tokens // 32
+    for chunk in range(chunks):
+        lax.fori_loop(chunk * 32, (chunk + 1) * 32, combine, 0, unroll=8)
+        for m in range(chunk * len(loads) // (chunks - 1), min((chunk + 1) * len(loads) // (chunks - 1), len(loads))):
+            loads[m].wait()
+            stores[m].start()
+        for b in (2 * chunk, 2 * chunk + 1):
+            at = slice(b * 16, (b + 1) * 16)
+            pair = jnp.concatenate([total3[at].reshape(256, LANES), back3[at].reshape(256, LANES)], axis=1)
+            turned = dot(turn[...], pair, NN).astype(BF)
+            for j in range(cols):
+                lanes = slice(j * LANES, (j + 1) * LANES)
+                lo[at, lanes] = turned[j * 16:(j + 1) * 16, :LANES]
+                gt[at, lanes] = turned[j * 16:(j + 1) * 16, LANES:]
     sums = jnp.sum(inner[...], axis=1, keepdims=True)
     spot = lax.broadcasted_iota(jnp.int32, (tokens, tokens), 0) == lax.broadcasted_iota(jnp.int32, (tokens, tokens), 1)
     for k in range(2):
-        routing[k:k + 1, :] = jnp.sum(
-            jnp.where(spot, sums[k * tokens:(k + 1) * tokens], 0.0), axis=0, keepdims=True)
-    for copy in moves:
+        product = jnp.sum(jnp.where(spot, sums[k * tokens:(k + 1) * tokens], 0.0), axis=0, keepdims=True)
+        routing[k:k + 1, :] = jnp.where(ftab[2 + k:3 + k, 0:tokens] > 0.0, product, 0.0)
+    for copy in stores:
         copy.wait()
 
 
@@ -462,19 +469,21 @@
         scratch_shapes=[
             pltpu.SMEM((8, 384), jnp.int32),
             pltpu.SMEM((8, 384), F32),
-            pltpu.VMEM(block, BF),
+            pltpu.VMEM((2 * CHIPS * cap, cols, LANES), BF),
             pltpu.VMEM((256, 256), BF),
             pltpu.VMEM((count, cols, LANES), F32),
             pltpu.VMEM((count, cols, LANES), BF),
             pltpu.VMEM((count, cols, LANES), BF),
             pltpu.VMEM((assigns, LANES), F32),
+            pltpu.VMEM((3, units, width), BF),
             dma((2,)),
             dma,
+            dma((3, pieces)),
             dma((3, pieces)),
         ],
         compiler_params=pltpu.CompilerParams(vmem_limit_bytes=62 * 1024 * 1024),
         cost_estimate=pl.CostEstimate(flops=0, bytes_accessed=12 * units * width, transcendentals=0),
-    )(grad_output, itab, ftab, ret, *grads)
+    )(grad_output, itab, ftab, ret.reshape(2 * CHIPS * cap, cols, LANES), *grads)
     return lo, gt, routing.T, gg, ug, dg
 
 

time: 377 us -> 98.2 us (0.26)
  Pallas kernels: 376 us -> 97.2 us
    pallas_call x1, Pallas kernels: 289 us -> 10.6 us  [body(): pl.pallas_call(functools.partial(last_kernel, cap, pieces), out_shape=(fl...]
where the time goes in v3:
time: 98.2 us; the launch traced here: 98 us
  Pallas kernels  97.2 us (99%)
    pallas_call x1, Pallas kernels, body(): pl.pallas_call(functools.partial(kernel, groups, cap), out_shape=(jax.Sha...  86.6 us
    pallas_call x1, Pallas kernels, body(): pl.pallas_call(functools.partial(last_kernel, cap, pieces), out_shape=(fl...  10.6 us

profile of v3, /device:TPU:1, one launch (start us, length us, event | category | flops | bytes accessed | tf_op | source)
XLA Modules:
  0.0 98.0 jit_solution(8193223871050335447)
XLA Ops:
  0.6 86.6 %shard_map.136 = (bf16[64,10,16,128]{3,2,1,0:T(8,128)(2,1)}, s32[8,384]{1,0:T(8,128)}, f32[8,384]{1,0:T(8,128)}, bf16[1,768,2048]{2,1,0:T(8,128)(2,1)}, bf16[1,7...) custom-call(s32[8]{0:T(128)} %swap.1, s32[4,16]{1,0:T(4,128)} %bitcast.6, s32[2,160]{1,0:T(2,128)} %bitcast.7, ...), custom_call_target="tpu_custom_call" | custom-call | flops 18119393280 | bytes 18874368 | tf_op jit(solution)/shard_map/pallas_call | solution.py:416
  87.2 10.6 %shard_map.137 = (bf16[160,2048]{1,0:T(8,128)(2,1)}, bf16[160,2048]{1,0:T(8,128)(2,1)}, f32[2,160]{1,0:T(2,128)}, bf16[1,768,2048]{2,1,0:T(8,128)(2,1)}, bf16[1,...) custom-call(bf16[160,2048]{1,0:T(8,128)(2,1)} %grad.3, s32[8,384]{1,0:T(8,128)} %get-tuple-element.18.itab, ...), custom_call_target="tpu_custom_call" | custom-call | bytes 18874368 | tf_op jit(solution)/shard_map/pallas_call | solution.py:464

commit v4 on v3

--- a/solution.py
+++ b/solution.py
@@ -93,7 +93,7 @@
            ret, itab, ftab, gg_hbm, ug_hbm, dg_hbm,
            itab_s, ftab_s, turn, tok3, grad3, send, recv, xs, ds, act, dgate, dup, ys, dxs, own, other, part,
            wg, wu, wd, act_t, dgate_t, dup_t, stage,
-           send_sem, recv_sem, fwd_ssem, fwd_rsem, part_ssem, part_rsem, ret_ssem, ret_rsem, w_sem, out_sem, tab_sem):
+           send_sem, recv_sem, fwd_ssem, fwd_rsem, part_ssem, part_rsem, ret_ssem, ret_rsem, w_sem, out_sem, tab_sem, round_sem):
     width = wg.shape[1]
     units = wg.shape[0]
     cols = width // LANES
@@ -116,11 +116,15 @@
     barrier = pltpu.get_barrier_semaphore()
     pl.semaphore_signal(barrier, inc=1, device_id=sibling, device_id_type=MESH)
 
-    def greet(n, _):
-        pl.semaphore_signal(barrier, inc=1, device_id=chip(n, 1), device_id_type=MESH)
-        return 0
-
-    lax.fori_loop(1, CHIPS, greet, 0)
+    def peer(i, j, k):
+        return {"expert": ((x + i) % SIDE) * SIDE + (z + j) % SIDE, "dp": ((y + k) % SIDE) * 2 + c}
+
+    for i in range(SIDE):
+        for j in range(SIDE):
+            if i or j:
+                pl.semaphore_signal(barrier, inc=1, device_id=peer(i, j, 0), device_id_type=MESH)
+    for k in range(1, SIDE):
+        pl.semaphore_signal(barrier, inc=1, device_id=peer(0, 0, k), device_id_type=MESH)
 
     def weight_copy(i):
         return pltpu.make_async_copy((wg_hbm, wu_hbm, wd_hbm)[i].at[0], (wg, wu, wd)[i], w_sem.at[i])
@@ -161,7 +165,10 @@
 
     gather(0, put_own)
 
-    pl.semaphore_wait(barrier, CHIPS)
+    pl.semaphore_wait(barrier, 19)
+    for k in range(1, SIDE):
+        pl.semaphore_signal(round_sem, inc=1, device_id=peer(0, 0, k), device_id_type=MESH)
+    pl.semaphore_wait(round_sem, 3)
 
     def send_rows(n, _):
         def put(r, value):
@@ -240,14 +247,14 @@
         lax.fori_loop(0, units // 256, hidden, 0)
 
         def model(n, _):
-            f = pl.ds(pl.multiple_of(n * 256, 256), 256)
+            f = pl.ds(pl.multiple_of(n * 512, 256), 512)
             out = dot(act[here, :], wd[:, f], NN)
             back = dot(dgate[here, :], wg[:, f], NN) + dot(dup[here, :], wu[:, f], NN)
             ys[:, f] = out.astype(BF)
             dxs[:, f] = back.astype(BF)
             return 0
 
-        lax.fori_loop(0, width // 256, model, 0)
+        lax.fori_loop(0, width // 512, model, 0)
         for p, dst in ((0, own), (1, other)):
             def pack(i, _):
                 n0 = first + i * 16
@@ -455,6 +462,7 @@
             dma((3,)),
             dma((2, 3)),
             dma((3,)),
+            pltpu.SemaphoreType.REGULAR,
         ],
         compiler_params=pltpu.CompilerParams(
             collective_id=0, has_side_effects=True, vmem_limit_bytes=62 * 1024 * 1024),

time: 98.2 us -> 95.3 us (0.970)
  Pallas kernels: 97.2 us -> 94.3 us
    pallas_call x1, Pallas kernels: 86.6 us -> 83.7 us  [body(): pl.pallas_call(functools.partial(kernel, groups, cap), out_shape=(jax.Sha...]
where the time goes in v4:
time: 95.3 us; the launch traced here: 95.1 us
  Pallas kernels  94.3 us (99%)
    pallas_call x1, Pallas kernels, body(): pl.pallas_call(functools.partial(kernel, groups, cap), out_shape=(jax.Sha...  83.7 us
    pallas_call x1, Pallas kernels, body(): pl.pallas_call(functools.partial(last_kernel, cap, pieces), out_shape=(fl...  10.6 us

profile of v4, /device:TPU:1, one launch (start us, length us, event | category | flops | bytes accessed | tf_op | source)
XLA Modules:
  0.0 95.1 jit_solution(13653793388343057477)
XLA Ops:
  0.6 83.7 %shard_map.136 = (bf16[64,10,16,128]{3,2,1,0:T(8,128)(2,1)}, s32[8,384]{1,0:T(8,128)}, f32[8,384]{1,0:T(8,128)}, bf16[1,768,2048]{2,1,0:T(8,128)(2,1)}, bf16[1,7...) custom-call(s32[8]{0:T(128)} %swap.1, s32[4,16]{1,0:T(4,128)} %bitcast.6, s32[2,160]{1,0:T(2,128)} %bitcast.7, ...), custom_call_target="tpu_custom_call" | custom-call | flops 18119393280 | bytes 18874368 | tf_op jit(solution)/shard_map/pallas_call | solution.py:423
  84.4 10.6 %shard_map.137 = (bf16[160,2048]{1,0:T(8,128)(2,1)}, bf16[160,2048]{1,0:T(8,128)(2,1)}, f32[2,160]{1,0:T(2,128)}, bf16[1,768,2048]{2,1,0:T(8,128)(2,1)}, bf16[1,...) custom-call(bf16[160,2048]{1,0:T(8,128)(2,1)} %grad.3, s32[8,384]{1,0:T(8,128)} %get-tuple-element.18.itab, ...), custom_call_target="tpu_custom_call" | custom-call | bytes 18874368 | tf_op jit(solution)/shard_map/pallas_call | solution.py:472

commit v5 on v4

--- a/solution.py
+++ b/solution.py
@@ -407,7 +407,7 @@
     cap = count * top // experts
     assigns = count * top
     cols = width // LANES
-    groups = 2
+    groups = 4
     pieces = 4
     slots = CHIPS // groups
     rows = 2 * slots * cap
@@ -450,7 +450,7 @@
             pltpu.VMEM((units, total), BF),
             pltpu.VMEM((units, total), BF),
             pltpu.VMEM((units, total), BF),
-            pltpu.VMEM((2, 3, units, 256), BF),
+            pltpu.VMEM((2, 3, units, 512), BF),
             dma((CHIPS,)),
             dma((CHIPS,)),
             dma((groups,)),

time: 95.3 us -> 90.6 us (0.951)
  Pallas kernels: 94.3 us -> 89.1 us
    pallas_call x1, Pallas kernels: 83.7 us -> 78.5 us  [body(): pl.pallas_call(functools.partial(kernel, groups, cap), out_shape=(jax.Sha...]
where the time goes in v5:
time: 90.6 us; the launch traced here: 89.9 us
  Pallas kernels  89.1 us (98%)
    pallas_call x1, Pallas kernels, body(): pl.pallas_call(functools.partial(kernel, groups, cap), out_shape=(jax.Sha...  78.5 us
    pallas_call x1, Pallas kernels, body(): pl.pallas_call(functools.partial(last_kernel, cap, pieces), out_shape=(fl...  10.6 us

profile of v5, /device:TPU:1, one launch (start us, length us, event | category | flops | bytes accessed | tf_op | source)
XLA Modules:
  0.0 89.9 jit_solution(15764119045650010736)
XLA Ops:
  0.6 78.5 %shard_map.136 = (bf16[64,10,16,128]{3,2,1,0:T(8,128)(2,1)}, s32[8,384]{1,0:T(8,128)}, f32[8,384]{1,0:T(8,128)}, bf16[1,768,2048]{2,1,0:T(8,128)(2,1)}, bf16[1,7...) custom-call(s32[8]{0:T(128)} %swap.1, s32[4,16]{1,0:T(4,128)} %bitcast.6, s32[2,160]{1,0:T(2,128)} %bitcast.7, ...), custom_call_target="tpu_custom_call" | custom-call | flops 18119393280 | bytes 18874368 | tf_op jit(solution)/shard_map/pallas_call | solution.py:423
  79.1 10.6 %shard_map.137 = (bf16[160,2048]{1,0:T(8,128)(2,1)}, bf16[160,2048]{1,0:T(8,128)(2,1)}, f32[2,160]{1,0:T(2,128)}, bf16[1,768,2048]{2,1,0:T(8,128)(2,1)}, bf16[1,...) custom-call(bf16[160,2048]{1,0:T(8,128)(2,1)} %grad.3, s32[8,384]{1,0:T(8,128)} %get-tuple-element.18.itab, ...), custom_call_target="tpu_custom_call" | custom-call | bytes 18874368 | tf_op jit(solution)/shard_map/pallas_call | solution.py:472
